TPU v7x, 1024 devices: a whole 4x8x16 slice. The times are simulated.
1024 devices in a mesh: row: 64 (over x, z_hi, y), col: 16 (over z_lo, core).
Axes of the slice: x: 4, y: 8, z: 16 (z_hi: 2, z_lo: 8; z = z_hi * 8 + z_lo), core: 2. Of those that a mesh axis runs over, the one named last changes fastest.
Arguments:
- blocks: float32 [2048, 8, 128, 128], P(('row', 'col')), as said below
- block_cols: int32 [2048, 8], P(('row', 'col')), may hold values from 0 to 2047, as said below
- pair_blocks: int32 [2048, 8, 8], P(('row', 'col')), may hold values from -1 to 2047, as said below
Outputs:
- purified: float32 [2048, 8, 128, 128], P(('row', 'col'))
Inputs may be any that keep to these rules, and one draw needn't show every extreme that they name: `block_cols`: row i's 8 columns are (i + d) modulo 2048 for 8 distinct d between -4 and 4, d = 0 always among them, listed in rising d; the pattern is symmetric: j is a column of row i exactly when i is a column of row j. `pair_blocks`: for block (i, s) with column j: every k such that both (i, k) and (k, j) are in the pattern, each once, in rising (k - i) modulo 2048 taken between -4 and 4, then -1s; every diagonal block lists 8 of them. `blocks`: the block at (j, i) is the transpose of the block at (i, j).
All inputs are finite; a program needn't handle non-finite values.
Results may differ from a plain program's by a relative error of at most 0.00005.
Values sent between devices are 32-bit elements; how exact they have to be, the bound alone decides.
No kernel may reach another device: no remote copies, remote signals or barrier semaphores. Data moves between devices by JAX's collectives and lax.ppermute only.
A program may use at most 64 MiB of HBM per device.

v0:
```python
import jax
import jax.numpy as jnp
from jax import lax
from jax.sharding import PartitionSpec as P

REACH = 4


def from_behind(value, axis, by):
    devices = lax.axis_size(axis)
    return lax.ppermute(value, axis, [(i, (i + by) % devices) for i in range(devices)])


def pick_slots(candidates, wanted):
    slot_range = jnp.arange(candidates.shape[-1], dtype=jnp.int32)
    return jnp.sum(jnp.where(candidates == wanted[..., None], slot_range, 0), axis=-1)


def on_device(blocks, block_cols, pair_blocks):
    rows_here = block_cols.shape[0]
    slot_count = block_cols.shape[1]
    size_block = blocks.shape[2]
    total_rows = rows_here * lax.axis_size(("row", "col"))
    first_row = lax.axis_index(("row", "col")) * rows_here
    hop_count = (REACH + rows_here - 1) // rows_here
    package = (blocks, block_cols.astype(jnp.float32))
    below_parts = []
    above_parts = []
    for hop_step in range(1, hop_count + 1):
        below_parts.insert(0, from_behind((package[0], package[1]), ("row", "col"), hop_step))
        above_parts.append(from_behind((package[0], package[1]), ("row", "col"), -hop_step))
    window_blocks = jnp.concatenate(
        [received[0] for received in below_parts]
        + [blocks]
        + [received[0] for received in above_parts],
        0,
    )
    window_cols = jnp.concatenate(
        [received[1] for received in below_parts]
        + [package[1]]
        + [received[1] for received in above_parts],
        0,
    )
    window_cols = window_cols.astype(jnp.int32)
    window_flat = window_blocks.reshape(-1, size_block, size_block)
    zero_index = window_flat.shape[0]
    padded_window = jnp.concatenate(
        [window_flat, jnp.zeros((1, size_block, size_block), jnp.float32)], 0
    )
    slot_rows = jnp.mod(block_cols - first_row + REACH, total_rows)
    slot_cols = window_cols[slot_rows]
    right_slot = pick_slots(
        slot_cols[:, None, :, :],
        jnp.broadcast_to(block_cols[:, :, None], (rows_here, slot_count, slot_count)),
    )
    listed = jnp.any(pair_blocks[:, :, None, :] == block_cols[:, None, :, None], axis=-1)
    right_index = jnp.where(listed, slot_rows[:, None, :] * slot_count + right_slot, zero_index)
    right_part = padded_window[right_index]
    square = jnp.einsum("iuab,isubc->isac", blocks, right_part, precision=lax.Precision.HIGHEST)
    cubed = jnp.einsum("iuab,isubc->isac", square, right_part, precision=lax.Precision.HIGHEST)
    return 3.0 * square - 2.0 * cubed


def solution(mesh):
    placed = (
        P(("row", "col"), None, None, None),
        P(("row", "col"), None),
        P(("row", "col"), None, None),
    )
    return jax.shard_map(
        on_device,
        mesh=mesh,
        in_specs=placed,
        out_specs=P(("row", "col"), None, None, None),
        check_vma=False,
    )
```

profile of v0, /device:TPU:990, one launch (start us, length us, event | category | flops | bytes accessed | tf_op | source)
XLA Modules:
  0.0 132.8 jit_solution(1447865118761481931)
XLA Ops:
  0.0 1.9 %collective-permute-start.1 = (f32[2,8,128,128]{3,2,1,0:T(8,128)}, f32[2,8,128,128]{3,2,1,0:T(8,128)S(1)}, u32[]{:S(2)}, u32[]{:S(2)}) collective-permute-start(f32[2,8,128,128]{3,2,1,0:T(8,128)} %param.3), channel_id=1, source_target_pairs={{0,1},{1,2},{2,3},{3,4},{4,5},{5,6},{6,7},{7,8},{8,9},{9,10},{10,1... | collective-permute-start | bytes 3145736 | tf_op jit(solution)/shard_map/ppermute | solution.py:11
  1.9 5.8 %collective-permute-start = (f32[2,8,128,128]{3,2,1,0:T(8,128)}, f32[2,8,128,128]{3,2,1,0:T(8,128)S(1)}, u32[]{:S(2)}, u32[]{:S(2)}) collective-permute-start(f32[2,8,128,128]{3,2,1,0:T(8,128)} %param.3), channel_id=1, source_target_pairs={{0,2},{1,3},{2,4},{3,5},{4,6},{5,7},{6,8},{7,9},{8,10},{9,11},{10,... | collective-permute-start | bytes 3145736 | tf_op jit(solution)/shard_map/ppermute | solution.py:11
  7.8 0.8 broadcast_multiply_fusion
  8.5 1.9 %collective-permute-start.7 = (f32[2,8]{1,0:T(2,128)S(1)}, f32[2,8]{1,0:T(2,128)S(1)}, u32[]{:S(2)}, u32[]{:S(2)}) collective-permute-start(f32[2,8]{1,0:T(2,128)S(1)} %get-tuple-element.7), channel_id=1, source_target_pairs={{0,1022},{1,1023},{2,0},{3,1},{4,2},{5,3},{6,4},{7,5},{8,6},{9,7},... | collective-permute-start | bytes 200 | tf_op jit(solution)/shard_map/ppermute | solution.py:11
  10.5 3.4 %collective-permute-start.6 = (f32[2,8]{1,0:T(2,128)S(1)}, f32[2,8]{1,0:T(2,128)S(1)}, u32[]{:S(2)}, u32[]{:S(2)}) collective-permute-start(f32[2,8]{1,0:T(2,128)S(1)} %get-tuple-element.7), channel_id=1, source_target_pairs={{0,1023},{1,0},{2,1},{3,2},{4,3},{5,4},{6,5},{7,6},{8,7},{9,8},{10... | collective-permute-start | bytes 200 | tf_op jit(solution)/shard_map/ppermute | solution.py:11
  13.8 1.9 %collective-permute-start.2 = (f32[2,8,128,128]{3,2,1,0:T(8,128)}, f32[2,8,128,128]{3,2,1,0:T(8,128)S(1)}, u32[]{:S(2)}, u32[]{:S(2)}) collective-permute-start(f32[2,8,128,128]{3,2,1,0:T(8,128)} %param.3), channel_id=1, source_target_pairs={{0,1023},{1,0},{2,1},{3,2},{4,3},{5,4},{6,5},{7,6},{8,7},{9,8},{10... | collective-permute-start | bytes 3145736 | tf_op jit(solution)/shard_map/ppermute | solution.py:11
  15.8 1.1 compare_reduce_fusion
  16.9 0.1 reshape.34
  17.0 16.6 %collective-permute-done.7 = f32[2,8]{1,0:T(2,128)S(1)} collective-permute-done((f32[2,8]{1,0:T(2,128)S(1)}, f32[2,8]{1,0:T(2,128)S(1)}, u32[]{:S(2)}, u32[]{:S(2)}) %collective-permute-start.7) | collective-permute-done | bytes 96 | tf_op jit(solution)/shard_map/ppermute | solution.py:11
  33.5 19.1 %collective-permute-start.5 = (f32[2,8]{1,0:T(2,128)S(1)}, f32[2,8]{1,0:T(2,128)S(1)}, u32[]{:S(2)}, u32[]{:S(2)}) collective-permute-start(f32[2,8]{1,0:T(2,128)S(1)} %get-tuple-element.7), channel_id=1, source_target_pairs={{0,1},{1,2},{2,3},{3,4},{4,5},{5,6},{6,7},{7,8},{8,9},{9,10},{10,1... | collective-permute-start | bytes 200 | tf_op jit(solution)/shard_map/ppermute | solution.py:11
  52.6 0.0 collective-permute-done.6
  52.6 1.9 %collective-permute-start.4 = (f32[2,8]{1,0:T(2,128)S(1)}, f32[2,8]{1,0:T(2,128)S(1)}, u32[]{:S(2)}, u32[]{:S(2)}) collective-permute-start(f32[2,8]{1,0:T(2,128)S(1)} %get-tuple-element.7), channel_id=1, source_target_pairs={{0,2},{1,3},{2,4},{3,5},{4,6},{5,7},{6,8},{7,9},{8,10},{9,11},{10,... | collective-permute-start | bytes 200 | tf_op jit(solution)/shard_map/ppermute | solution.py:11
  54.6 0.0 collective-permute-done.5
  54.6 3.9 %collective-permute-start.3 = (f32[2,8,128,128]{3,2,1,0:T(8,128)}, f32[2,8,128,128]{3,2,1,0:T(8,128)}, u32[]{:S(2)}, u32[]{:S(2)}) collective-permute-start(f32[2,8,128,128]{3,2,1,0:T(8,128)} %param.3), channel_id=1, source_target_pairs={{0,1022},{1,1023},{2,0},{3,1},{4,2},{5,3},{6,4},{7,5},{8,6},{9,7},... | collective-permute-start | bytes 3145736 | tf_op jit(solution)/shard_map/ppermute | solution.py:11
  58.5 0.0 collective-permute-done.4
  58.6 0.6 gather_fusion
  59.1 1.1 select_reduce_fusion
  60.3 0.1 reshape.42
  60.4 0.0 collective-permute-done
  60.4 0.1 constant_dynamic-update-slice_fusion.4
  60.4 0.0 collective-permute-done.1
  60.5 0.1 constant_dynamic-update-slice_fusion.3
  60.5 1.3 constant_dynamic-update-slice_fusion.2
  61.8 0.0 collective-permute-done.2
  61.9 0.1 constant_dynamic-update-slice_fusion.1
  61.9 28.6 %collective-permute-done.3 = f32[2,8,128,128]{3,2,1,0:T(8,128)} collective-permute-done((f32[2,8,128,128]{3,2,1,0:T(8,128)}, f32[2,8,128,128]{3,2,1,0:T(8,128)}, u32[]{:S(2)}, u32[]{:S(2)}) %collective-permute-start.3) | collective-permute-done | bytes 1048608 | tf_op jit(solution)/shard_map/ppermute | solution.py:11
  90.6 1.3 constant_dynamic-update-slice_fusion
  91.9 3.0 %concatenate.10 = f32[81,128,128]{2,1,0:T(8,128)} pad(f32[80,128,128]{2,1,0:T(8,128)S(1)} %bitcast.52, f32[]{:T(128)} %constant.17.clone.1), padding=0_1x0_0x0_0 | pad | bytes 10551300 | tf_op jit(solution)/shard_map/concatenate | solution.py:47
  94.9 0.0 copy-start.1
  94.9 6.9 %gather_fusion.1 = f32[128,128,128]{2,1,0:T(8,128)} fusion(f32[81,128,128]{2,1,0:T(8,128)} %concatenate.10, s32[1024]{0:T(1024)S(1)} %pad_clamp_fusion), kind=kCustom, calls=%fused_computation.1 | custom fusion | bytes 16777728 | tf_op jit(solution)/shard_map/gather | solution.py:58
  101.8 0.0 copy-done.1
  101.8 0.0 copy-start
  101.8 16.5 %fusion.4 = f32[2,8,128,128,1]{3,2,4,1,0:T(8,128)S(1)} fusion(f32[2,8,8,128,128]{4,3,2,1,0:T(8,128)} %bitcast.50, f32[2,8,128,128]{3,2,1,0:T(8,128)S(1)} %copy-done.1), kind=kOutput, calls=%fused_computation.7 | convolution fusion | flops 3221225472 | bytes 10485760 | tf_op jit(solution)/shard_map/iuab,isubc->isac/dot_general | solution.py:59
  118.4 0.0 copy-done
  118.4 13.1 %fusion.2 = f32[2,8,128,128]{2,3,1,0:T(8,128)S(1)} fusion(f32[2,8,8,128,128]{4,3,2,1,0:T(8,128)S(1)} %bitcast.51, f32[2,8,128,128,1]{3,2,4,1,0:T(8,128)S(1)} %fusion.4), kind=kOutput, calls=%fused_computation.5 | convolution fusion | flops 3222011904 | bytes 10485760 | tf_op jit(solution)/shard_map/iuab,isubc->isac/dot_general | solution.py:60
  131.5 1.3 copy.13
  (6 shorter events, 0.1 us)
Async XLA Ops:
  0.0 60.4 %collective-permute-start.1 = (f32[2,8,128,128]{3,2,1,0:T(8,128)}, f32[2,8,128,128]{3,2,1,0:T(8,128)S(1)}, u32[]{:S(2)}, u32[]{:S(2)}) collective-permute-start(f32[2,8,128,128]{3,2,1,0:T(8,128)} %param.3), channel_id=1, source_target_pairs={{0,1},{1,2},{2,3},{3,4},{4,5},{5,6},{6,7},{7,8},{8,9},{9,10},{10,1... | collective-permute-start | bytes 3145736 | tf_op jit(solution)/shard_map/ppermute | solution.py:11
  1.9 58.4 %collective-permute-start = (f32[2,8,128,128]{3,2,1,0:T(8,128)}, f32[2,8,128,128]{3,2,1,0:T(8,128)S(1)}, u32[]{:S(2)}, u32[]{:S(2)}) collective-permute-start(f32[2,8,128,128]{3,2,1,0:T(8,128)} %param.3), channel_id=1, source_target_pairs={{0,2},{1,3},{2,4},{3,5},{4,6},{5,7},{6,8},{7,9},{8,10},{9,11},{10,... | collective-permute-start | bytes 3145736 | tf_op jit(solution)/shard_map/ppermute | solution.py:11
  8.5 25.0 %collective-permute-start.7 = (f32[2,8]{1,0:T(2,128)S(1)}, f32[2,8]{1,0:T(2,128)S(1)}, u32[]{:S(2)}, u32[]{:S(2)}) collective-permute-start(f32[2,8]{1,0:T(2,128)S(1)} %get-tuple-element.7), channel_id=1, source_target_pairs={{0,1022},{1,1023},{2,0},{3,1},{4,2},{5,3},{6,4},{7,5},{8,6},{9,7},... | collective-permute-start | bytes 200 | tf_op jit(solution)/shard_map/ppermute | solution.py:11
  10.5 42.2 %collective-permute-start.6 = (f32[2,8]{1,0:T(2,128)S(1)}, f32[2,8]{1,0:T(2,128)S(1)}, u32[]{:S(2)}, u32[]{:S(2)}) collective-permute-start(f32[2,8]{1,0:T(2,128)S(1)} %get-tuple-element.7), channel_id=1, source_target_pairs={{0,1023},{1,0},{2,1},{3,2},{4,3},{5,4},{6,5},{7,6},{8,7},{9,8},{10... | collective-permute-start | bytes 200 | tf_op jit(solution)/shard_map/ppermute | solution.py:11
  13.8 48.0 %collective-permute-start.2 = (f32[2,8,128,128]{3,2,1,0:T(8,128)}, f32[2,8,128,128]{3,2,1,0:T(8,128)S(1)}, u32[]{:S(2)}, u32[]{:S(2)}) collective-permute-start(f32[2,8,128,128]{3,2,1,0:T(8,128)} %param.3), channel_id=1, source_target_pairs={{0,1023},{1,0},{2,1},{3,2},{4,3},{5,4},{6,5},{7,6},{8,7},{9,8},{10... | collective-permute-start | bytes 3145736 | tf_op jit(solution)/shard_map/ppermute | solution.py:11
  33.5 21.0 %collective-permute-start.5 = (f32[2,8]{1,0:T(2,128)S(1)}, f32[2,8]{1,0:T(2,128)S(1)}, u32[]{:S(2)}, u32[]{:S(2)}) collective-permute-start(f32[2,8]{1,0:T(2,128)S(1)} %get-tuple-element.7), channel_id=1, source_target_pairs={{0,1},{1,2},{2,3},{3,4},{4,5},{5,6},{6,7},{7,8},{8,9},{9,10},{10,1... | collective-permute-start | bytes 200 | tf_op jit(solution)/shard_map/ppermute | solution.py:11
  52.6 5.9 %collective-permute-start.4 = (f32[2,8]{1,0:T(2,128)S(1)}, f32[2,8]{1,0:T(2,128)S(1)}, u32[]{:S(2)}, u32[]{:S(2)}) collective-permute-start(f32[2,8]{1,0:T(2,128)S(1)} %get-tuple-element.7), channel_id=1, source_target_pairs={{0,2},{1,3},{2,4},{3,5},{4,6},{5,7},{6,8},{7,9},{8,10},{9,11},{10,... | collective-permute-start | bytes 200 | tf_op jit(solution)/shard_map/ppermute | solution.py:11
  54.6 36.0 %collective-permute-start.3 = (f32[2,8,128,128]{3,2,1,0:T(8,128)}, f32[2,8,128,128]{3,2,1,0:T(8,128)}, u32[]{:S(2)}, u32[]{:S(2)}) collective-permute-start(f32[2,8,128,128]{3,2,1,0:T(8,128)} %param.3), channel_id=1, source_target_pairs={{0,1022},{1,1023},{2,0},{3,1},{4,2},{5,3},{6,4},{7,5},{8,6},{9,7},... | collective-permute-start | bytes 3145736 | tf_op jit(solution)/shard_map/ppermute | solution.py:11
  94.9 6.9 %copy-start.1 = (f32[2,8,128,128]{3,2,1,0:T(8,128)S(1)}, f32[2,8,128,128]{3,2,1,0:T(8,128)}, u32[]{:S(2)}) copy-start(f32[2,8,128,128]{3,2,1,0:T(8,128)} %param.3) | copy-start | bytes 3145732
  101.8 16.5 %copy-start = (f32[128,128,128]{2,1,0:T(8,128)S(1)}, f32[128,128,128]{2,1,0:T(8,128)}, u32[]{:S(2)}) copy-start(f32[128,128,128]{2,1,0:T(8,128)} %gather_fusion.1) | copy-start | bytes 25165828
where the time goes:
time: 133 us
  waiting for transfers between devices  45.2 us (34%)
  starting transfers between devices  39.9 us (30%)
  matrix products  29.7 us (22%)
  local copies, waits for them, and re-layouts  14.8 us (11%)
  other arithmetic  3.02 us (2%)
    ppermute x8, waiting for transfers between devices, from_behind(): lax.ppermute(value, axis, [(i, (i + by) % devices) for i in range(devices)])  45.2 us
    ppermute x8, starting transfers between devices, from_behind(): lax.ppermute(value, axis, [(i, (i + by) % devices) for i in range(devices)])  39.9 us
    dot_general x1, matrix products, on_device(): jnp.einsum('iuab,isubc->isac', blocks, right_part, precision=lax.Precisio...  16.5 us
    dot_general x1, matrix products, on_device(): jnp.einsum('iuab,isubc->isac', square, right_part, precision=lax.Precisio...  13.1 us
    gather x1, local copies, waits for them, and re-layouts, on_device(): right_part = padded_window[right_index]  6.9 us
    concatenate x1, local copies, waits for them, and re-layouts, on_device(): jnp.concatenate([window_flat, jnp.zeros((1, size_block, size_block), jnp....  3.05 us
  transfers between devices with their start and end apart: 8, of which 2 were waited for; matrix products, arithmetic and copies ran while one was open for 4% of the time, Pallas kernels for 0%

commit v1 on v0

v1 whole, which is shorter than its diff:
```python
import jax
import jax.numpy as jnp
from jax import lax
from jax.experimental import pallas as pl
from jax.experimental.pallas import tpu as pltpu
from jax.sharding import PartitionSpec as P

B = 128
NNZ = 8
REACH = 4
ROWS = 2
SPAN = ROWS + 2 * REACH
PAIR = 2 * B
AXES = ("row", "col")
PACKED = 2 * B + 8
DOWN = PACKED + 4 * B
UP = DOWN + 3 * B
NEAR1, NEAR2 = DOWN + 16, DOWN + 8
LATE = 4
BF, F32 = jnp.bfloat16, jnp.float32
SMEM = pl.BlockSpec(memory_space=pltpu.SMEM)
VMEM = pl.BlockSpec(memory_space=pltpu.VMEM)
ANY = pl.BlockSpec(memory_space=pl.ANY)


def device_index():
    return lax.axis_index("row") * lax.axis_size("col") + lax.axis_index("col")


def missing_of(cols_ref, first_row, total_rows):
    found = []
    for i in range(ROWS):
        count = jnp.int32(0)
        for s in range(NNZ):
            natural = lax.rem(first_row + i + s - REACH + total_rows, total_rows)
            count = count + jnp.where(cols_ref[i, s] == natural, 1, 0)
        found.append(count)
    return found


def held(missing, offset):
    return offset != missing


def slot_of(missing, offset):
    return jnp.minimum(offset - jnp.where(missing < offset, 1, 0), NNZ - 1)


def own_block(blocks_ref, missing, i, offset):
    value = blocks_ref[i, slot_of(missing[i], offset)]
    return jnp.where(held(missing[i], offset), value, 0.0)


def grid_ids():
    return lax.broadcasted_iota(jnp.int32, (B, B), 0), lax.broadcasted_iota(jnp.int32, (B, B), 1)


def write_triangle(blocks_ref, missing, out_ref):
    first = own_block(blocks_ref, missing, 0, REACH)
    second = own_block(blocks_ref, missing, 1, REACH)
    rows, cols = grid_ids()
    out_ref[0:B] = jnp.where(rows <= cols, first, second)
    out_ref[B : 2 * B] = own_block(blocks_ref, missing, 0, REACH + 1)
    diagonal = jnp.sum(jnp.where(rows == cols, second, 0.0), axis=0, keepdims=True)
    out_ref[2 * B : PACKED] = jnp.broadcast_to(diagonal, (PACKED - 2 * B, B))


def read_triangle(ref):
    packed, between = ref[0:B], ref[B : 2 * B]
    turned = packed.T
    rows, cols = grid_ids()
    first = jnp.where(rows <= cols, packed, turned)
    second = jnp.where(rows > cols, packed, jnp.where(rows < cols, turned, ref[2 * B : 2 * B + 1]))
    return first, between, second


def pack_up(
    total_rows, blocks_hbm, cols_hbm, up_ref, tri_ref, blocks_ref, cols_ref, blocks_sem, cols_sem
):
    fetch_cols = pltpu.make_async_copy(cols_hbm, cols_ref, cols_sem)
    fetch_blocks = pltpu.make_async_copy(blocks_hbm, blocks_ref, blocks_sem)
    fetch_cols.start()
    fetch_blocks.start()
    fetch_cols.wait()
    missing = missing_of(cols_ref, device_index() * ROWS, total_rows)
    fetch_blocks.wait()
    write_triangle(blocks_ref, missing, tri_ref)
    up_ref[0:PACKED] = tri_ref[...]
    below = ((0, -2), (0, -1), (1, -2), (1, -1))
    across = ((1, 4), (1, 5), (0, 4))
    for n, (i, j) in enumerate(below + across):
        at = PACKED + n * B
        up_ref[at : at + B] = own_block(blocks_ref, missing, i, j - i + REACH)


def pack_down(
    total_rows, blocks_ref, cols_ref, tri_in_ref, near1_ref, near2_ref, last1_ref, last2_ref
):
    missing = missing_of(cols_ref, device_index() * ROWS, total_rows)
    for ref in (near1_ref, near2_ref, last1_ref, last2_ref):
        ref[0:PACKED] = tri_in_ref[...]
    for n, (i, j) in enumerate(((0, 2), (0, 3), (1, 2), (1, 3))):
        at = PACKED + n * B
        value = own_block(blocks_ref, missing, i, j - i + REACH)
        near1_ref[at : at + B] = value
        last1_ref[at : at + B] = value


def pass_on(up1_ref, up2_ref, up1_out_ref, up2_out_ref):
    pass


def tile(n):
    return slice(n * B, (n + 1) * B)


def purify(
    total_rows,
    blocks_ref,
    cols_ref,
    up1_ref,
    up2_ref,
    down1_ref,
    down2_ref,
    out_hbm,
    high,
    low,
    square,
    square_high,
    square_low,
    staged,
    out_sem,
):
    missing = missing_of(cols_ref, device_index() * ROWS, total_rows)

    def put(k, j, value):
        top = value.astype(BF)
        high[tile(k), tile(j)] = top
        low[tile(k), tile(j)] = (value - top.astype(F32)).astype(BF)

    def put_both(k, j, value):
        put(k, j, value)
        put(j, k, value.T)

    for i in range(ROWS):
        for offset in range(2 * REACH + 1):
            value = own_block(blocks_ref, missing, i, offset)
            j = i + offset
            if REACH <= j < REACH + ROWS:
                put(REACH + i, j, value)
            else:
                put_both(REACH + i, j, value)
    for ref, at in ((up2_ref, 0), (up1_ref, 2), (down1_ref, 6), (down2_ref, 8)):
        first, between, second = read_triangle(ref)
        put(at, at, first)
        put_both(at, at + 1, between)
        put(at + 1, at + 1, second)
    for n, (k, j) in enumerate(((2, 0), (2, 1), (3, 0), (3, 1))):
        put_both(k, j, up1_ref[PACKED + n * B : PACKED + (n + 1) * B])
    for n, (k, j) in enumerate(((6, 8), (6, 9), (7, 8), (7, 9))):
        put_both(k, j, down1_ref[PACKED + n * B : PACKED + (n + 1) * B])
    for n, (k, j) in enumerate(((3, 6), (3, 7), (2, 6))):
        put_both(k, j, up1_ref[DOWN + n * B : DOWN + (n + 1) * B])
    nothing = jnp.zeros((B, B), BF)
    for k, j in ((0, 5), (2, 7), (4, 9)):
        for part in (high, low):
            part[tile(k), tile(j)] = nothing
            part[tile(j), tile(k)] = nothing

    def product(left_high, left_low, b):
        inner = slice(max(0, b - 2) * PAIR, min(SPAN // 2, b + 3) * PAIR)
        outer = slice(b * PAIR, (b + 1) * PAIR)

        def dot(left, right):
            return jnp.dot(left, right[inner, outer], preferred_element_type=F32)

        return dot(left_high(inner), high) + dot(left_low(inner), high) + dot(left_high(inner), low)

    own = slice(REACH * B, (REACH + ROWS) * B)
    for b in range(SPAN // 2):
        total = product(lambda at: high[own, at], lambda at: low[own, at], b)
        for i in range(ROWS):
            for j in (2 * b, 2 * b + 1):
                value = total[tile(i), tile(j - 2 * b)]
                offset = j - i
                if 0 <= offset <= 2 * REACH:
                    value = jnp.where(held(missing[i], offset), value, 0.0)
                else:
                    value = jnp.zeros_like(value)
                square[tile(i), tile(j)] = value
                top = value.astype(BF)
                square_high[tile(i), tile(j)] = top
                square_low[tile(i), tile(j)] = (value - top.astype(F32)).astype(BF)
    for b in range(SPAN // 2):
        total = product(lambda at: square_high[:, at], lambda at: square_low[:, at], b)
        outer = slice(b * PAIR, (b + 1) * PAIR)
        square[:, outer] = 3.0 * square[:, outer] - 2.0 * total
        for i in range(ROWS):
            for s in range(NNZ):
                if (i + s + 1) // 2 == b:
                    at = pl.multiple_of((i + s + jnp.where(missing[i] <= s, 1, 0)) * B, B)
                    staged[i, s] = square[tile(i), pl.ds(at, B)]
                    pltpu.make_async_copy(staged.at[i, s], out_hbm.at[i, s], out_sem).start()
    pltpu.make_async_copy(staged, out_hbm, out_sem).wait()


def late():
    return lax.axis_index("col") >= lax.axis_size("col") - LATE


def purify_most(total_rows, *refs):
    @pl.when(jnp.logical_not(late()))
    def _():
        purify(total_rows, *refs)


def purify_last(
    total_rows,
    blocks_ref,
    cols_ref,
    up1_ref,
    up2_ref,
    down1_ref,
    down2_ref,
    last1_ref,
    last2_ref,
    given_ref,
    *refs,
):
    @pl.when(late())
    def _():
        @pl.when(lax.axis_index("col") == lax.axis_size("col") - 1)
        def _():
            down1_ref[0:DOWN] = last1_ref[...]

        down2_ref[0:PACKED] = last2_ref[...]
        purify(
            total_rows, blocks_ref, cols_ref, up1_ref, up2_ref, down1_ref, down2_ref, *refs
        )


def shifted(value, by):
    devices = lax.axis_size(AXES)
    return lax.ppermute(value, AXES, [(d, (d + by) % devices) for d in range(devices)])


def shifted_down(value, by, near):
    devices, run = lax.axis_size(AXES), lax.axis_size("col")
    inside = range(1, run) if by == 1 else range(2, run - 2)
    pairs = [(d, (d - by) % devices) for d in range(devices) if (d % run in inside) == near]
    return lax.ppermute(value, AXES, pairs)


def on_device(blocks, block_cols, pair_blocks):
    total_rows = ROWS * lax.axis_size(AXES)
    f32 = lambda *shape: jax.ShapeDtypeStruct(shape, F32)
    params = pltpu.CompilerParams(vmem_limit_bytes=48 << 20)
    hbm = pl.BlockSpec(memory_space=pltpu.HBM)
    up, triangle, blocks = pl.pallas_call(
        lambda *refs: pack_up(total_rows, *refs),
        out_shape=(f32(UP, B), f32(PACKED, B), f32(ROWS, NNZ, B, B)),
        in_specs=[hbm, hbm],
        out_specs=(VMEM, VMEM, VMEM),
        scratch_shapes=[
            pltpu.SMEM((ROWS, NNZ), jnp.int32),
            pltpu.SemaphoreType.DMA,
            pltpu.SemaphoreType.DMA,
        ],
        compiler_params=params,
        name="pack_up",
    )(blocks, block_cols)
    up1 = shifted(up, 1)
    up2 = shifted(triangle, 2)
    near1, near2, last1, last2 = pl.pallas_call(
        lambda *refs: pack_down(total_rows, *refs),
        out_shape=(f32(NEAR1, B), f32(NEAR2, B), f32(DOWN, B), f32(PACKED, B)),
        in_specs=[VMEM, SMEM, VMEM],
        out_specs=(VMEM,) * 4,
        compiler_params=params,
        name="pack_down",
    )(blocks, block_cols, triangle)
    down1 = shifted_down(near1, 1, True)
    down2 = shifted_down(near2, 2, True)
    last1 = shifted_down(last1, 1, False)
    last2 = shifted_down(last2, 2, False)
    up1, up2 = pl.pallas_call(
        pass_on,
        out_shape=(f32(UP, B), f32(PACKED, B)),
        in_specs=[ANY] * 2,
        out_specs=(ANY,) * 2,
        input_output_aliases={0: 0, 1: 1},
        compiler_params=params,
        cost_estimate=pl.CostEstimate(flops=4_000_000_000, bytes_accessed=1024, transcendentals=0),
        name="pass_on",
    )(up1, up2)
    window = pltpu.VMEM((SPAN * B, SPAN * B), BF)
    strip = pltpu.VMEM((ROWS * B, SPAN * B), BF)
    work = [window, window, pltpu.VMEM((ROWS * B, SPAN * B), F32), strip, strip]
    work += [pltpu.VMEM((ROWS, NNZ, B, B), F32), pltpu.SemaphoreType.DMA]
    result = pl.pallas_call(
        lambda *refs: purify_most(total_rows, *refs),
        out_shape=f32(ROWS, NNZ, B, B),
        in_specs=[VMEM, SMEM] + [VMEM] * 4,
        out_specs=ANY,
        scratch_shapes=work,
        compiler_params=params,
        name="purify_most",
    )(blocks, block_cols, up1, up2, down1, down2)
    return pl.pallas_call(
        lambda *refs: purify_last(total_rows, *refs),
        out_shape=f32(ROWS, NNZ, B, B),
        in_specs=[VMEM, SMEM] + [VMEM] * 6 + [ANY],
        out_specs=ANY,
        input_output_aliases={8: 0},
        scratch_shapes=work,
        compiler_params=params,
        name="purify_last",
    )(blocks, block_cols, up1, up2, down1, down2, last1, last2, result)


def solution(mesh):
    placed = (
        P(AXES, None, None, None),
        P(AXES, None),
        P(AXES, None, None),
    )
    return jax.shard_map(
        on_device,
        mesh=mesh,
        in_specs=placed,
        out_specs=P(AXES, None, None, None),
        check_vma=False,
    )
```

time: 133 us -> 47.5 us (0.36)
  the two profiles are of different devices: /device:TPU:990 before, /device:TPU:1 now
where the time goes in v1:
time: 47.5 us; the launch traced here: 47.2 us
  starting transfers between devices  25.8 us (54%)
  waiting for transfers between devices  11.5 us (24%)
  Pallas kernels  7.89 us (17%)
  local copies, waits for them, and re-layouts  1.9 us (4%)
    ppermute x4, starting transfers between devices, shifted_down(): return lax.ppermute(value, AXES, pairs)  16.4 us
    ppermute x2, waiting for transfers between devices, shifted(): lax.ppermute(value, AXES, [(d, (d + by) % devices) for d in range(devices)])  11.5 us
    ppermute x2, starting transfers between devices, shifted(): lax.ppermute(value, AXES, [(d, (d + by) % devices) for d in range(devices)])  9.39 us
    pallas_call x1, Pallas kernels, on_device(): pl.pallas_call(lambda *refs: purify_most(total_rows, *refs), out_shape=f3...  5.97 us
    unnamed x4, local copies, waits for them, and re-layouts  1.9 us
  transfers between devices with their start and end apart: 6, of which 1 were waited for; matrix products, arithmetic and copies ran while one was open for 0% of the time, Pallas kernels for 14%

profile of v1, /device:TPU:1, one launch (start us, length us, event | category | flops | bytes accessed | tf_op | source)
XLA Modules:
  0.0 47.2 jit_solution(2591553769594050816)
XLA Ops:
  0.0 0.0 copy-start
  0.0 1.2 %copy-done = f32[2,8,128,128]{3,2,1,0:T(8,128)S(1)} copy-done((f32[2,8,128,128]{3,2,1,0:T(8,128)S(1)}, f32[2,8,128,128]{3,2,1,0:T(8,128)}, u32[]{:S(2)}) %copy-start) | copy-done | bytes 1048600
  1.2 0.0 copy-start.1
  1.2 0.7 %copy-done.1 = s32[2,8]{1,0:T(2,128)S(1)} copy-done((s32[2,8]{1,0:T(2,128)S(1)}, s32[2,8]{1,0:T(2,128)}, u32[]{:S(2)}) %copy-start.1) | copy-done | bytes 88
  1.9 0.7 %pack_up.1 = (f32[1160,128]{1,0:T(8,128)S(1)}, f32[264,128]{1,0:T(8,128)S(1)}, f32[2,8,128,128]{3,2,1,0:T(8,128)S(1)}) custom-call(f32[2,8,128,128]{3,2,1,0:T(8,128)S(1)} %copy-done, s32[2,8]{1,0:T(2,128)S(1)} %copy-done.1), custom_call_target="tpu_custom_call" | custom-call | tf_op jit(solution)/shard_map/pack_up/pallas_call | solution.py:259
  2.6 5.4 %collective-permute-start = (f32[1160,128]{1,0:T(8,128)S(1)}, f32[1160,128]{1,0:T(8,128)S(1)}, u32[]{:S(2)}, u32[]{:S(2)}) collective-permute-start(f32[1160,128]{1,0:T(8,128)S(1)} %get-tuple-element.15), channel_id=1, source_target_pairs={{0,1},{1,2},{2,3},{3,4},{4,5},{5,6},{6,7},{7,8},{8,9},{9,10},{10,1... | collective-permute-start | bytes 1781768 | tf_op jit(solution)/shard_map/ppermute | solution.py:244
  8.0 4.0 %collective-permute-start.1 = (f32[264,128]{1,0:T(8,128)S(1)}, f32[264,128]{1,0:T(8,128)S(1)}, u32[]{:S(2)}, u32[]{:S(2)}) collective-permute-start(f32[264,128]{1,0:T(8,128)S(1)} %get-tuple-element.16.refs_2_), channel_id=1, source_target_pairs={{0,2},{1,3},{2,4},{3,5},{4,6},{5,7},{6,8},{7,9},{8,10},{9,11},{10,... | collective-permute-start | bytes 405512 | tf_op jit(solution)/shard_map/ppermute | solution.py:244
  12.0 0.6 %pack_down.1 = (f32[792,128]{1,0:T(8,128)S(1)}, f32[784,128]{1,0:T(8,128)S(1)}, f32[776,128]{1,0:T(8,128)S(1)}, f32[264,128]{1,0:T(8,128)S(1)}) custom-call(f32[2,8,128,128]{3,2,1,0:T(8,128)S(1)} %get-tuple-element.14.refs_0_, s32[2,8]{1,0:T(2,128)S(1)} %copy-done.1, f32[264,128]{1,0:T(8,128)S(1)} %get-tuple-element.16.refs_2_), custom_call_target="tpu_custom_call" | custom-call | tf_op jit(solution)/shard_map/pack_down/pallas_call | solution.py:274
  12.7 10.5 %collective-permute-start.2 = (f32[792,128]{1,0:T(8,128)S(1)}, f32[792,128]{1,0:T(8,128)S(1)}, u32[]{:S(2)}, u32[]{:S(2)}) collective-permute-start(f32[792,128]{1,0:T(8,128)S(1)} %get-tuple-element.19), channel_id=1, source_target_pairs={{1,0},{2,1},{3,2},{4,3},{5,4},{6,5},{7,6},{8,7},{9,8},{10,9},{11,1... | collective-permute-start | bytes 1216520 | tf_op jit(solution)/shard_map/ppermute | solution.py:251
  23.2 1.3 %collective-permute-start.3 = (f32[784,128]{1,0:T(8,128)S(1)}, f32[784,128]{1,0:T(8,128)S(1)}, u32[]{:S(2)}, u32[]{:S(2)}) collective-permute-start(f32[784,128]{1,0:T(8,128)S(1)} %get-tuple-element.20), channel_id=1, source_target_pairs={{2,0},{3,1},{4,2},{5,3},{6,4},{7,5},{8,6},{9,7},{10,8},{11,9},{12,... | collective-permute-start | bytes 1204232 | tf_op jit(solution)/shard_map/ppermute | solution.py:251
  24.5 0.7 %collective-permute-start.4 = (f32[776,128]{1,0:T(8,128)S(1)}, f32[776,128]{1,0:T(8,128)S(1)}, u32[]{:S(2)}, u32[]{:S(2)}) collective-permute-start(f32[776,128]{1,0:T(8,128)S(1)} %get-tuple-element.21), channel_id=1, source_target_pairs={{0,1023},{16,15},{32,31},{48,47},{64,63},{80,79},{96,95},{112,111}... | collective-permute-start | bytes 1191944 | tf_op jit(solution)/shard_map/ppermute | solution.py:251
  25.2 11.5 %collective-permute-done.1.up2_ref = f32[264,128]{1,0:T(8,128)S(1)} collective-permute-done((f32[264,128]{1,0:T(8,128)S(1)}, f32[264,128]{1,0:T(8,128)S(1)}, u32[]{:S(2)}, u32[]{:S(2)}) %collective-permute-start.1) | collective-permute-done | bytes 135200 | tf_op jit(solution)/shard_map/ppermute | solution.py:244
  36.7 3.9 %collective-permute-start.5 = (f32[264,128]{1,0:T(8,128)S(1)}, f32[264,128]{1,0:T(8,128)S(1)}, u32[]{:S(2)}, u32[]{:S(2)}) collective-permute-start(f32[264,128]{1,0:T(8,128)S(1)} %get-tuple-element.22), channel_id=1, source_target_pairs={{0,1022},{1,1023},{14,12},{15,13},{16,14},{17,15},{30,28},{31,29},... | collective-permute-start | bytes 405512 | tf_op jit(solution)/shard_map/ppermute | solution.py:251
  40.6 0.0 collective-permute-done.up1_ref
  40.6 0.0 collective-permute-done.3.refs_5_
  40.6 0.0 collective-permute-done.2.refs_4_
  40.7 6.0 %purify_most.1.refs_8_ = f32[2,8,128,128]{3,2,1,0:T(8,128)} custom-call(f32[2,8,128,128]{3,2,1,0:T(8,128)S(1)} %get-tuple-element.14.refs_0_, s32[2,8]{1,0:T(2,128)S(1)} %copy-done.1, f32[1160,128]{1,0:T(8,128)S(1)} %get-tuple-element.17.refs_2_, f32[264,128]{1,0:T(8,128)S(1)} %get-tuple-element.18.refs_3_, f32[792,128]{1,0:T(8,128)S(1)} %collective-permute-done.2.refs_4_, ...), custom_call_target="tpu_custom_call" | custom-call | tf_op jit(solution)/shard_map/purify_most/pallas_call | solution.py:300
  46.6 0.0 collective-permute-done.5.refs_7_
  46.6 0.0 collective-permute-done.4.refs_6_
  46.7 0.6 %purify_last.1 = f32[2,8,128,128]{3,2,1,0:T(8,128)} custom-call(f32[2,8,128,128]{3,2,1,0:T(8,128)S(1)} %get-tuple-element.14.refs_0_, s32[2,8]{1,0:T(2,128)S(1)} %copy-done.1, f32[1160,128]{1,0:T(8,128)S(1)} %get-tuple-element.17.refs_2_, f32[264,128]{1,0:T(8,128)S(1)} %get-tuple-element.18.refs_3_, ...), custom_call_target="tpu_custom_call", output_to_operand_aliasing={{}: (8, {})} | custom-call | tf_op jit(solution)/shard_map/purify_last/pallas_call | solution.py:309
  (1 shorter events, 0.0 us)
Async XLA Ops:
  0.0 1.2 %copy-start = (f32[2,8,128,128]{3,2,1,0:T(8,128)S(1)}, f32[2,8,128,128]{3,2,1,0:T(8,128)}, u32[]{:S(2)}) copy-start(f32[2,8,128,128]{3,2,1,0:T(8,128)} %refs_0_.1) | copy-start | bytes 3145732
  1.2 0.7 %copy-start.1 = (s32[2,8]{1,0:T(2,128)S(1)}, s32[2,8]{1,0:T(2,128)}, u32[]{:S(2)}) copy-start(s32[2,8]{1,0:T(2,128)} %refs_1_.7) | copy-start | bytes 196
  2.6 38.0 %collective-permute-start = (f32[1160,128]{1,0:T(8,128)S(1)}, f32[1160,128]{1,0:T(8,128)S(1)}, u32[]{:S(2)}, u32[]{:S(2)}) collective-permute-start(f32[1160,128]{1,0:T(8,128)S(1)} %get-tuple-element.15), channel_id=1, source_target_pairs={{0,1},{1,2},{2,3},{3,4},{4,5},{5,6},{6,7},{7,8},{8,9},{9,10},{10,1... | collective-permute-start | bytes 1781768 | tf_op jit(solution)/shard_map/ppermute | solution.py:244
  8.0 28.7 %collective-permute-start.1 = (f32[264,128]{1,0:T(8,128)S(1)}, f32[264,128]{1,0:T(8,128)S(1)}, u32[]{:S(2)}, u32[]{:S(2)}) collective-permute-start(f32[264,128]{1,0:T(8,128)S(1)} %get-tuple-element.16.refs_2_), channel_id=1, source_target_pairs={{0,2},{1,3},{2,4},{3,5},{4,6},{5,7},{6,8},{7,9},{8,10},{9,11},{10,... | collective-permute-start | bytes 405512 | tf_op jit(solution)/shard_map/ppermute | solution.py:244
  12.7 28.0 %collective-permute-start.2 = (f32[792,128]{1,0:T(8,128)S(1)}, f32[792,128]{1,0:T(8,128)S(1)}, u32[]{:S(2)}, u32[]{:S(2)}) collective-permute-start(f32[792,128]{1,0:T(8,128)S(1)} %get-tuple-element.19), channel_id=1, source_target_pairs={{1,0},{2,1},{3,2},{4,3},{5,4},{6,5},{7,6},{8,7},{9,8},{10,9},{11,1... | collective-permute-start | bytes 1216520 | tf_op jit(solution)/shard_map/ppermute | solution.py:251
  23.2 17.4 %collective-permute-start.3 = (f32[784,128]{1,0:T(8,128)S(1)}, f32[784,128]{1,0:T(8,128)S(1)}, u32[]{:S(2)}, u32[]{:S(2)}) collective-permute-start(f32[784,128]{1,0:T(8,128)S(1)} %get-tuple-element.20), channel_id=1, source_target_pairs={{2,0},{3,1},{4,2},{5,3},{6,4},{7,5},{8,6},{9,7},{10,8},{11,9},{12,... | collective-permute-start | bytes 1204232 | tf_op jit(solution)/shard_map/ppermute | solution.py:251
  24.5 22.2 %collective-permute-start.4 = (f32[776,128]{1,0:T(8,128)S(1)}, f32[776,128]{1,0:T(8,128)S(1)}, u32[]{:S(2)}, u32[]{:S(2)}) collective-permute-start(f32[776,128]{1,0:T(8,128)S(1)} %get-tuple-element.21), channel_id=1, source_target_pairs={{0,1023},{16,15},{32,31},{48,47},{64,63},{80,79},{96,95},{112,111}... | collective-permute-start | bytes 1191944 | tf_op jit(solution)/shard_map/ppermute | solution.py:251
  36.7 9.9 %collective-permute-start.5 = (f32[264,128]{1,0:T(8,128)S(1)}, f32[264,128]{1,0:T(8,128)S(1)}, u32[]{:S(2)}, u32[]{:S(2)}) collective-permute-start(f32[264,128]{1,0:T(8,128)S(1)} %get-tuple-element.22), channel_id=1, source_target_pairs={{0,1022},{1,1023},{14,12},{15,13},{16,14},{17,15},{30,28},{31,29},... | collective-permute-start | bytes 405512 | tf_op jit(solution)/shard_map/ppermute | solution.py:251

commit v2 on v1

--- a/solution.py
+++ b/solution.py
@@ -15,7 +15,6 @@
 PACKED = 2 * B + 8
 DOWN = PACKED + 4 * B
 UP = DOWN + 3 * B
-NEAR1, NEAR2 = DOWN + 16, DOWN + 8
 LATE = 4
 BF, F32 = jnp.bfloat16, jnp.float32
 SMEM = pl.BlockSpec(memory_space=pltpu.SMEM)
@@ -38,6 +37,10 @@
     return found
 
 
+def known(missing_ref):
+    return [missing_ref[i, 0] for i in range(ROWS)]
+
+
 def held(missing, offset):
     return offset != missing
 
@@ -75,7 +78,7 @@
 
 
 def pack_up(
-    total_rows, blocks_hbm, cols_hbm, up_ref, tri_ref, blocks_ref, cols_ref, blocks_sem, cols_sem
+    total_rows, blocks_hbm, cols_hbm, up_ref, tri_ref, blocks_ref, missing_ref, cols_ref, blocks_sem, cols_sem
 ):
     fetch_cols = pltpu.make_async_copy(cols_hbm, cols_ref, cols_sem)
     fetch_blocks = pltpu.make_async_copy(blocks_hbm, blocks_ref, blocks_sem)
@@ -83,6 +86,8 @@
     fetch_blocks.start()
     fetch_cols.wait()
     missing = missing_of(cols_ref, device_index() * ROWS, total_rows)
+    for i in range(ROWS):
+        missing_ref[i : i + 1] = jnp.full((1, B), missing[i], jnp.int32)
     fetch_blocks.wait()
     write_triangle(blocks_ref, missing, tri_ref)
     up_ref[0:PACKED] = tri_ref[...]
@@ -93,17 +98,18 @@
         up_ref[at : at + B] = own_block(blocks_ref, missing, i, j - i + REACH)
 
 
-def pack_down(
-    total_rows, blocks_ref, cols_ref, tri_in_ref, near1_ref, near2_ref, last1_ref, last2_ref
-):
-    missing = missing_of(cols_ref, device_index() * ROWS, total_rows)
-    for ref in (near1_ref, near2_ref, last1_ref, last2_ref):
+def pack_down(blocks_ref, missing_ref, tri_in_ref, down1_ref, down2_ref):
+    missing = known(missing_ref)
+    for ref in (down1_ref, down2_ref):
         ref[0:PACKED] = tri_in_ref[...]
     for n, (i, j) in enumerate(((0, 2), (0, 3), (1, 2), (1, 3))):
         at = PACKED + n * B
         value = own_block(blocks_ref, missing, i, j - i + REACH)
-        near1_ref[at : at + B] = value
-        last1_ref[at : at + B] = value
+        down1_ref[at : at + B] = value
+
+
+def pass_four(*refs):
+    pass
 
 
 def pass_on(up1_ref, up2_ref, up1_out_ref, up2_out_ref):
@@ -115,9 +121,8 @@
 
 
 def purify(
-    total_rows,
     blocks_ref,
-    cols_ref,
+    missing_ref,
     up1_ref,
     up2_ref,
     down1_ref,
@@ -131,7 +136,7 @@
     staged,
     out_sem,
 ):
-    missing = missing_of(cols_ref, device_index() * ROWS, total_rows)
+    missing = known(missing_ref)
 
     def put(k, j, value):
         top = value.astype(BF)
@@ -208,16 +213,15 @@
     return lax.axis_index("col") >= lax.axis_size("col") - LATE
 
 
-def purify_most(total_rows, *refs):
+def purify_most(*refs):
     @pl.when(jnp.logical_not(late()))
     def _():
-        purify(total_rows, *refs)
+        purify(*refs)
 
 
 def purify_last(
-    total_rows,
     blocks_ref,
-    cols_ref,
+    missing_ref,
     up1_ref,
     up2_ref,
     down1_ref,
@@ -229,13 +233,15 @@
 ):
     @pl.when(late())
     def _():
-        @pl.when(lax.axis_index("col") == lax.axis_size("col") - 1)
+        col = lax.axis_index("col") - lax.axis_size("col")
+
+        @pl.when(col == -1)
         def _():
-            down1_ref[0:DOWN] = last1_ref[...]
-
-        down2_ref[0:PACKED] = last2_ref[...]
+            down1_ref[...] = last1_ref[...]
+
+        down2_ref[...] = last2_ref[...]
         purify(
-            total_rows, blocks_ref, cols_ref, up1_ref, up2_ref, down1_ref, down2_ref, *refs
+            blocks_ref, missing_ref, up1_ref, up2_ref, down1_ref, down2_ref, *refs
         )
 
 
@@ -256,11 +262,16 @@
     f32 = lambda *shape: jax.ShapeDtypeStruct(shape, F32)
     params = pltpu.CompilerParams(vmem_limit_bytes=48 << 20)
     hbm = pl.BlockSpec(memory_space=pltpu.HBM)
-    up, triangle, blocks = pl.pallas_call(
+    up, triangle, blocks, missing = pl.pallas_call(
         lambda *refs: pack_up(total_rows, *refs),
-        out_shape=(f32(UP, B), f32(PACKED, B), f32(ROWS, NNZ, B, B)),
+        out_shape=(
+            f32(UP, B),
+            f32(PACKED, B),
+            f32(ROWS, NNZ, B, B),
+            jax.ShapeDtypeStruct((8, B), jnp.int32),
+        ),
         in_specs=[hbm, hbm],
-        out_specs=(VMEM, VMEM, VMEM),
+        out_specs=(VMEM,) * 4,
         scratch_shapes=[
             pltpu.SMEM((ROWS, NNZ), jnp.int32),
             pltpu.SemaphoreType.DMA,
@@ -271,18 +282,27 @@
     )(blocks, block_cols)
     up1 = shifted(up, 1)
     up2 = shifted(triangle, 2)
-    near1, near2, last1, last2 = pl.pallas_call(
-        lambda *refs: pack_down(total_rows, *refs),
-        out_shape=(f32(NEAR1, B), f32(NEAR2, B), f32(DOWN, B), f32(PACKED, B)),
-        in_specs=[VMEM, SMEM, VMEM],
-        out_specs=(VMEM,) * 4,
+    send1, send2 = pl.pallas_call(
+        pack_down,
+        out_shape=(f32(DOWN, B), f32(PACKED, B)),
+        in_specs=[VMEM] * 3,
+        out_specs=(VMEM,) * 2,
         compiler_params=params,
         name="pack_down",
-    )(blocks, block_cols, triangle)
-    down1 = shifted_down(near1, 1, True)
-    down2 = shifted_down(near2, 2, True)
-    last1 = shifted_down(last1, 1, False)
-    last2 = shifted_down(last2, 2, False)
+    )(blocks, missing, triangle)
+    down1 = shifted_down(send1, 1, True)
+    down2 = shifted_down(send2, 2, True)
+    down1, down2, send1, send2 = pl.pallas_call(
+        pass_four,
+        out_shape=tuple(f32(n, B) for n in (DOWN, PACKED, DOWN, PACKED)),
+        in_specs=[ANY] * 4,
+        out_specs=(ANY,) * 4,
+        input_output_aliases={n: n for n in range(4)},
+        compiler_params=params,
+        name="pass_four",
+    )(down1, down2, send1, send2)
+    last1 = shifted_down(send1, 1, False)
+    last2 = shifted_down(send2, 2, False)
     up1, up2 = pl.pallas_call(
         pass_on,
         out_shape=(f32(UP, B), f32(PACKED, B)),
@@ -298,24 +318,24 @@
     work = [window, window, pltpu.VMEM((ROWS * B, SPAN * B), F32), strip, strip]
     work += [pltpu.VMEM((ROWS, NNZ, B, B), F32), pltpu.SemaphoreType.DMA]
     result = pl.pallas_call(
-        lambda *refs: purify_most(total_rows, *refs),
+        purify_most,
         out_shape=f32(ROWS, NNZ, B, B),
-        in_specs=[VMEM, SMEM] + [VMEM] * 4,
+        in_specs=[VMEM] * 6,
         out_specs=ANY,
         scratch_shapes=work,
         compiler_params=params,
         name="purify_most",
-    )(blocks, block_cols, up1, up2, down1, down2)
+    )(blocks, missing, up1, up2, down1, down2)
     return pl.pallas_call(
-        lambda *refs: purify_last(total_rows, *refs),
+        purify_last,
         out_shape=f32(ROWS, NNZ, B, B),
-        in_specs=[VMEM, SMEM] + [VMEM] * 6 + [ANY],
+        in_specs=[VMEM] * 8 + [ANY],
         out_specs=ANY,
         input_output_aliases={8: 0},
         scratch_shapes=work,
         compiler_params=params,
         name="purify_last",
-    )(blocks, block_cols, up1, up2, down1, down2, last1, last2, result)
+    )(blocks, missing, up1, up2, down1, down2, last1, last2, result)
 
 
 def solution(mesh):

time: 47.5 us -> 43.4 us (0.914)
  the two profiles are of different devices: /device:TPU:1 before, /device:TPU:990 now
where the time goes in v2:
time: 43.4 us; the launch traced here: 43.1 us
  starting transfers between devices  21.5 us (50%)
  waiting for transfers between devices  13.3 us (31%)
  Pallas kernels  6.29 us (14%)
  local copies, waits for them, and re-layouts  1.9 us (4%)
    ppermute x4, starting transfers between devices, shifted_down(): return lax.ppermute(value, AXES, pairs)  15.4 us
    ppermute x4, waiting for transfers between devices, shifted_down(): return lax.ppermute(value, AXES, pairs)  13.3 us
    ppermute x2, starting transfers between devices, shifted(): lax.ppermute(value, AXES, [(d, (d + by) % devices) for d in range(devices)])  6.02 us
    pallas_call x1, Pallas kernels, on_device(): pl.pallas_call(purify_last, out_shape=f32(ROWS, NNZ, B, B), in_specs=[VME...  5.49 us
    unnamed x4, local copies, waits for them, and re-layouts  1.9 us
  transfers between devices with their start and end apart: 6, of which 2 were waited for; matrix products, arithmetic and copies ran while one was open for 0% of the time, Pallas kernels for 0%

profile of v2, /device:TPU:990, one launch (start us, length us, event | category | flops | bytes accessed | tf_op | source)
XLA Modules:
  0.0 43.1 jit_solution(4591341352888287507)
XLA Ops:
  0.0 0.0 copy-start
  0.0 1.2 %copy-done = f32[2,8,128,128]{3,2,1,0:T(8,128)S(1)} copy-done((f32[2,8,128,128]{3,2,1,0:T(8,128)S(1)}, f32[2,8,128,128]{3,2,1,0:T(8,128)}, u32[]{:S(2)}) %copy-start) | copy-done | bytes 1048600
  1.2 0.0 copy-start.1
  1.2 0.7 %copy-done.1 = s32[2,8]{1,0:T(2,128)S(1)} copy-done((s32[2,8]{1,0:T(2,128)S(1)}, s32[2,8]{1,0:T(2,128)}, u32[]{:S(2)}) %copy-start.1) | copy-done | bytes 88
  1.9 0.7 %pack_up.1 = (f32[1160,128]{1,0:T(8,128)S(1)}, f32[264,128]{1,0:T(8,128)S(1)}, f32[2,8,128,128]{3,2,1,0:T(8,128)S(1)}, s32[8,128]{1,0:T(8,128)S(1)}) custom-call(f32[2,8,128,128]{3,2,1,0:T(8,128)S(1)} %copy-done, s32[2,8]{1,0:T(2,128)S(1)} %copy-done.1), custom_call_target="tpu_custom_call" | custom-call | tf_op jit(solution)/shard_map/pack_up/pallas_call | solution.py:265
  2.6 1.9 %collective-permute-start = (f32[1160,128]{1,0:T(8,128)S(1)}, f32[1160,128]{1,0:T(8,128)S(1)}, u32[]{:S(2)}, u32[]{:S(2)}) collective-permute-start(f32[1160,128]{1,0:T(8,128)S(1)} %get-tuple-element.19), channel_id=1, source_target_pairs={{0,1},{1,2},{2,3},{3,4},{4,5},{5,6},{6,7},{7,8},{8,9},{9,10},{10,1... | collective-permute-start | bytes 1781768 | tf_op jit(solution)/shard_map/ppermute | solution.py:250
  4.5 0.1 pack_down.1
  4.6 3.6 %collective-permute-start.2 = (f32[776,128]{1,0:T(8,128)S(1)}, f32[776,128]{1,0:T(8,128)S(1)}, u32[]{:S(2)}, u32[]{:S(2)}) collective-permute-start(f32[776,128]{1,0:T(8,128)S(1)} %get-tuple-element.23.refs_2_), channel_id=1, source_target_pairs={{1,0},{2,1},{3,2},{4,3},{5,4},{6,5},{7,6},{8,7},{9,8},{10,9},{11,1... | collective-permute-start | bytes 1191944 | tf_op jit(solution)/shard_map/ppermute | solution.py:257
  8.3 0.7 %collective-permute-start.3 = (f32[264,128]{1,0:T(8,128)S(1)}, f32[264,128]{1,0:T(8,128)S(1)}, u32[]{:S(2)}, u32[]{:S(2)}) collective-permute-start(f32[264,128]{1,0:T(8,128)S(1)} %get-tuple-element.24.refs_3_), channel_id=1, source_target_pairs={{2,0},{3,1},{4,2},{5,3},{6,4},{7,5},{8,6},{9,7},{10,8},{11,9},{12,... | collective-permute-start | bytes 405512 | tf_op jit(solution)/shard_map/ppermute | solution.py:257
  9.0 4.1 %collective-permute-start.1 = (f32[264,128]{1,0:T(8,128)S(1)}, f32[264,128]{1,0:T(8,128)S(1)}, u32[]{:S(2)}, u32[]{:S(2)}) collective-permute-start(f32[264,128]{1,0:T(8,128)S(1)} %get-tuple-element.20.tri_in_ref), channel_id=1, source_target_pairs={{0,2},{1,3},{2,4},{3,5},{4,6},{5,7},{6,8},{7,9},{8,10},{9,11},{10,... | collective-permute-start | bytes 405512 | tf_op jit(solution)/shard_map/ppermute | solution.py:250
  13.1 0.0 collective-permute-done.3.refs_1_
  13.1 4.7 %collective-permute-done.2.refs_0_ = f32[776,128]{1,0:T(8,128)S(1)} collective-permute-done((f32[776,128]{1,0:T(8,128)S(1)}, f32[776,128]{1,0:T(8,128)S(1)}, u32[]{:S(2)}, u32[]{:S(2)}) %collective-permute-start.2) | collective-permute-done | bytes 397344 | tf_op jit(solution)/shard_map/ppermute | solution.py:257
  17.8 0.7 %collective-permute-start.4 = (f32[776,128]{1,0:T(8,128)S(1)}, f32[776,128]{1,0:T(8,128)S(1)}, u32[]{:S(2)}, u32[]{:S(2)}) collective-permute-start(f32[776,128]{1,0:T(8,128)S(1)} %get-tuple-element.27), channel_id=1, source_target_pairs={{0,1023},{16,15},{32,31},{48,47},{64,63},{80,79},{96,95},{112,111}... | collective-permute-start | bytes 1191944 | tf_op jit(solution)/shard_map/ppermute | solution.py:257
  18.4 10.5 %collective-permute-start.5 = (f32[264,128]{1,0:T(8,128)S(1)}, f32[264,128]{1,0:T(8,128)S(1)}, u32[]{:S(2)}, u32[]{:S(2)}) collective-permute-start(f32[264,128]{1,0:T(8,128)S(1)} %get-tuple-element.28), channel_id=1, source_target_pairs={{0,1022},{1,1023},{14,12},{15,13},{16,14},{17,15},{30,28},{31,29},... | collective-permute-start | bytes 405512 | tf_op jit(solution)/shard_map/ppermute | solution.py:257
  28.9 0.0 collective-permute-done.1.up2_ref
  28.9 0.0 collective-permute-done.up1_ref
  29.0 8.7 %collective-permute-done.5.last2_ref = f32[264,128]{1,0:T(8,128)S(1)} collective-permute-done((f32[264,128]{1,0:T(8,128)S(1)}, f32[264,128]{1,0:T(8,128)S(1)}, u32[]{:S(2)}, u32[]{:S(2)}) %collective-permute-start.5) | collective-permute-done | bytes 135200 | tf_op jit(solution)/shard_map/ppermute | solution.py:257
  37.6 0.0 collective-permute-done.4.last1_ref
  37.6 5.5 %purify_last.1 = f32[2,8,128,128]{3,2,1,0:T(8,128)} custom-call(f32[2,8,128,128]{3,2,1,0:T(8,128)S(1)} %get-tuple-element.17.blocks_ref.refs_0_, s32[8,128]{1,0:T(8,128)S(1)} %get-tuple-element.18.missing_ref.refs_1_, f32[1160,128]{1,0:T(8,128)S(1)} %get-tuple-element.21.refs_2_.up1_ref, ...), custom_call_target="tpu_custom_call", output_to_operand_aliasing={{}: (8, {})} | custom-call | tf_op jit(solution)/shard_map/purify_last/pallas_call | solution.py:329
  (3 shorter events, 0.0 us)
Async XLA Ops:
  0.0 1.2 %copy-start = (f32[2,8,128,128]{3,2,1,0:T(8,128)S(1)}, f32[2,8,128,128]{3,2,1,0:T(8,128)}, u32[]{:S(2)}) copy-start(f32[2,8,128,128]{3,2,1,0:T(8,128)} %refs_0_.1) | copy-start | bytes 3145732
  1.2 0.7 %copy-start.1 = (s32[2,8]{1,0:T(2,128)S(1)}, s32[2,8]{1,0:T(2,128)}, u32[]{:S(2)}) copy-start(s32[2,8]{1,0:T(2,128)} %refs_1_.1) | copy-start | bytes 196
  2.6 26.3 %collective-permute-start = (f32[1160,128]{1,0:T(8,128)S(1)}, f32[1160,128]{1,0:T(8,128)S(1)}, u32[]{:S(2)}, u32[]{:S(2)}) collective-permute-start(f32[1160,128]{1,0:T(8,128)S(1)} %get-tuple-element.19), channel_id=1, source_target_pairs={{0,1},{1,2},{2,3},{3,4},{4,5},{5,6},{6,7},{7,8},{8,9},{9,10},{10,1... | collective-permute-start | bytes 1781768 | tf_op jit(solution)/shard_map/ppermute | solution.py:250
  4.6 13.1 %collective-permute-start.2 = (f32[776,128]{1,0:T(8,128)S(1)}, f32[776,128]{1,0:T(8,128)S(1)}, u32[]{:S(2)}, u32[]{:S(2)}) collective-permute-start(f32[776,128]{1,0:T(8,128)S(1)} %get-tuple-element.23.refs_2_), channel_id=1, source_target_pairs={{1,0},{2,1},{3,2},{4,3},{5,4},{6,5},{7,6},{8,7},{9,8},{10,9},{11,1... | collective-permute-start | bytes 1191944 | tf_op jit(solution)/shard_map/ppermute | solution.py:257
  8.3 4.8 %collective-permute-start.3 = (f32[264,128]{1,0:T(8,128)S(1)}, f32[264,128]{1,0:T(8,128)S(1)}, u32[]{:S(2)}, u32[]{:S(2)}) collective-permute-start(f32[264,128]{1,0:T(8,128)S(1)} %get-tuple-element.24.refs_3_), channel_id=1, source_target_pairs={{2,0},{3,1},{4,2},{5,3},{6,4},{7,5},{8,6},{9,7},{10,8},{11,9},{12,... | collective-permute-start | bytes 405512 | tf_op jit(solution)/shard_map/ppermute | solution.py:257
  9.0 20.0 %collective-permute-start.1 = (f32[264,128]{1,0:T(8,128)S(1)}, f32[264,128]{1,0:T(8,128)S(1)}, u32[]{:S(2)}, u32[]{:S(2)}) collective-permute-start(f32[264,128]{1,0:T(8,128)S(1)} %get-tuple-element.20.tri_in_ref), channel_id=1, source_target_pairs={{0,2},{1,3},{2,4},{3,5},{4,6},{5,7},{6,8},{7,9},{8,10},{9,11},{10,... | collective-permute-start | bytes 405512 | tf_op jit(solution)/shard_map/ppermute | solution.py:250
  17.8 19.9 %collective-permute-start.4 = (f32[776,128]{1,0:T(8,128)S(1)}, f32[776,128]{1,0:T(8,128)S(1)}, u32[]{:S(2)}, u32[]{:S(2)}) collective-permute-start(f32[776,128]{1,0:T(8,128)S(1)} %get-tuple-element.27), channel_id=1, source_target_pairs={{0,1023},{16,15},{32,31},{48,47},{64,63},{80,79},{96,95},{112,111}... | collective-permute-start | bytes 1191944 | tf_op jit(solution)/shard_map/ppermute | solution.py:257
  18.4 19.2 %collective-permute-start.5 = (f32[264,128]{1,0:T(8,128)S(1)}, f32[264,128]{1,0:T(8,128)S(1)}, u32[]{:S(2)}, u32[]{:S(2)}) collective-permute-start(f32[264,128]{1,0:T(8,128)S(1)} %get-tuple-element.28), channel_id=1, source_target_pairs={{0,1022},{1,1023},{14,12},{15,13},{16,14},{17,15},{30,28},{31,29},... | collective-permute-start | bytes 405512 | tf_op jit(solution)/shard_map/ppermute | solution.py:257

commit v3 on v2

--- a/solution.py
+++ b/solution.py
@@ -77,18 +77,10 @@
     return first, between, second
 
 
-def pack_up(
-    total_rows, blocks_hbm, cols_hbm, up_ref, tri_ref, blocks_ref, missing_ref, cols_ref, blocks_sem, cols_sem
-):
-    fetch_cols = pltpu.make_async_copy(cols_hbm, cols_ref, cols_sem)
-    fetch_blocks = pltpu.make_async_copy(blocks_hbm, blocks_ref, blocks_sem)
-    fetch_cols.start()
-    fetch_blocks.start()
-    fetch_cols.wait()
+def pack_up(total_rows, blocks_ref, cols_ref, up_ref, tri_ref, missing_ref):
     missing = missing_of(cols_ref, device_index() * ROWS, total_rows)
     for i in range(ROWS):
         missing_ref[i : i + 1] = jnp.full((1, B), missing[i], jnp.int32)
-    fetch_blocks.wait()
     write_triangle(blocks_ref, missing, tri_ref)
     up_ref[0:PACKED] = tri_ref[...]
     below = ((0, -2), (0, -1), (1, -2), (1, -1))
@@ -261,22 +253,11 @@
     total_rows = ROWS * lax.axis_size(AXES)
     f32 = lambda *shape: jax.ShapeDtypeStruct(shape, F32)
     params = pltpu.CompilerParams(vmem_limit_bytes=48 << 20)
-    hbm = pl.BlockSpec(memory_space=pltpu.HBM)
-    up, triangle, blocks, missing = pl.pallas_call(
+    up, triangle, missing = pl.pallas_call(
         lambda *refs: pack_up(total_rows, *refs),
-        out_shape=(
-            f32(UP, B),
-            f32(PACKED, B),
-            f32(ROWS, NNZ, B, B),
-            jax.ShapeDtypeStruct((8, B), jnp.int32),
-        ),
-        in_specs=[hbm, hbm],
-        out_specs=(VMEM,) * 4,
-        scratch_shapes=[
-            pltpu.SMEM((ROWS, NNZ), jnp.int32),
-            pltpu.SemaphoreType.DMA,
-            pltpu.SemaphoreType.DMA,
-        ],
+        out_shape=(f32(UP, B), f32(PACKED, B), jax.ShapeDtypeStruct((8, B), jnp.int32)),
+        in_specs=[VMEM, VMEM],
+        out_specs=(VMEM,) * 3,
         compiler_params=params,
         name="pack_up",
     )(blocks, block_cols)

time: 43.4 us -> 42.9 us (0.988)
  the two profiles are of different devices: /device:TPU:990 before, /device:TPU:984 now
where the time goes in v3:
time: 42.9 us; the launch traced here: 42.6 us
  starting transfers between devices  21.6 us (50%)
  waiting for transfers between devices  13.2 us (31%)
  Pallas kernels  5.79 us (13%)
  local copies, waits for them, and re-layouts  1.91 us (4%)
    ppermute x4, starting transfers between devices, shifted_down(): return lax.ppermute(value, AXES, pairs)  15.6 us
    ppermute x4, waiting for transfers between devices, shifted_down(): return lax.ppermute(value, AXES, pairs)  13.2 us
    ppermute x2, starting transfers between devices, shifted(): lax.ppermute(value, AXES, [(d, (d + by) % devices) for d in range(devices)])  6.02 us
    pallas_call x1, Pallas kernels, on_device(): pl.pallas_call(purify_last, out_shape=f32(ROWS, NNZ, B, B), in_specs=[VME...  5.48 us
    unnamed x6, local copies, waits for them, and re-layouts  1.91 us
  transfers between devices with their start and end apart: 6, of which 2 were waited for; matrix products, arithmetic and copies ran while one was open for 0% of the time, Pallas kernels for 0%

profile of v3, /device:TPU:984, one launch (start us, length us, event | category | flops | bytes accessed | tf_op | source)
XLA Modules:
  0.0 42.6 jit_solution(10108909497642305373)
XLA Ops:
  0.0 0.0 copy-start
  0.0 1.2 %copy-done = f32[2,8,128,128]{3,2,1,0:T(8,128)S(1)} copy-done((f32[2,8,128,128]{3,2,1,0:T(8,128)S(1)}, f32[2,8,128,128]{3,2,1,0:T(8,128)}, u32[]{:S(2)}) %copy-start) | copy-done | bytes 1048600
  1.2 0.0 copy-start.2
  1.2 0.7 %copy-done.2 = s32[2,8]{1,0:T(2,128)S(1)} copy-done((s32[2,8]{1,0:T(2,128)S(1)}, s32[2,8]{1,0:T(2,128)}, u32[]{:S(2)}) %copy-start.2) | copy-done | bytes 88
  1.9 0.2 pack_up.1
  2.1 1.9 %collective-permute-start = (f32[1160,128]{1,0:T(8,128)S(1)}, f32[1160,128]{1,0:T(8,128)S(1)}, u32[]{:S(2)}, u32[]{:S(2)}) collective-permute-start(f32[1160,128]{1,0:T(8,128)S(1)} %get-tuple-element.17), channel_id=1, source_target_pairs={{0,1},{1,2},{2,3},{3,4},{4,5},{5,6},{6,7},{7,8},{8,9},{9,10},{10,1... | collective-permute-start | bytes 1781768 | tf_op jit(solution)/shard_map/ppermute | solution.py:242
  4.0 0.1 pack_down.1
  4.1 3.6 %collective-permute-start.2 = (f32[776,128]{1,0:T(8,128)S(1)}, f32[776,128]{1,0:T(8,128)S(1)}, u32[]{:S(2)}, u32[]{:S(2)}) collective-permute-start(f32[776,128]{1,0:T(8,128)S(1)} %get-tuple-element.21.refs_2_), channel_id=1, source_target_pairs={{1,0},{2,1},{3,2},{4,3},{5,4},{6,5},{7,6},{8,7},{9,8},{10,9},{11,1... | collective-permute-start | bytes 1191944 | tf_op jit(solution)/shard_map/ppermute | solution.py:249
  7.8 0.7 %collective-permute-start.3 = (f32[264,128]{1,0:T(8,128)S(1)}, f32[264,128]{1,0:T(8,128)S(1)}, u32[]{:S(2)}, u32[]{:S(2)}) collective-permute-start(f32[264,128]{1,0:T(8,128)S(1)} %get-tuple-element.22.refs_3_), channel_id=1, source_target_pairs={{2,0},{3,1},{4,2},{5,3},{6,4},{7,5},{8,6},{9,7},{10,8},{11,9},{12,... | collective-permute-start | bytes 405512 | tf_op jit(solution)/shard_map/ppermute | solution.py:249
  8.5 4.1 %collective-permute-start.1 = (f32[264,128]{1,0:T(8,128)S(1)}, f32[264,128]{1,0:T(8,128)S(1)}, u32[]{:S(2)}, u32[]{:S(2)}) collective-permute-start(f32[264,128]{1,0:T(8,128)S(1)} %get-tuple-element.18.tri_in_ref), channel_id=1, source_target_pairs={{0,2},{1,3},{2,4},{3,5},{4,6},{5,7},{6,8},{7,9},{8,10},{9,11},{10,... | collective-permute-start | bytes 405512 | tf_op jit(solution)/shard_map/ppermute | solution.py:242
  12.6 0.0 collective-permute-done.3.refs_1_
  12.6 4.7 %collective-permute-done.2.refs_0_ = f32[776,128]{1,0:T(8,128)S(1)} collective-permute-done((f32[776,128]{1,0:T(8,128)S(1)}, f32[776,128]{1,0:T(8,128)S(1)}, u32[]{:S(2)}, u32[]{:S(2)}) %collective-permute-start.2) | collective-permute-done | bytes 397344 | tf_op jit(solution)/shard_map/ppermute | solution.py:249
  17.3 0.7 %collective-permute-start.4 = (f32[776,128]{1,0:T(8,128)S(1)}, f32[776,128]{1,0:T(8,128)S(1)}, u32[]{:S(2)}, u32[]{:S(2)}) collective-permute-start(f32[776,128]{1,0:T(8,128)S(1)} %get-tuple-element.25), channel_id=1, source_target_pairs={{0,1023},{16,15},{32,31},{48,47},{64,63},{80,79},{96,95},{112,111}... | collective-permute-start | bytes 1191944 | tf_op jit(solution)/shard_map/ppermute | solution.py:249
  17.9 0.0 copy-start.1
  18.0 10.6 %collective-permute-start.5 = (f32[264,128]{1,0:T(8,128)S(1)}, f32[264,128]{1,0:T(8,128)S(1)}, u32[]{:S(2)}, u32[]{:S(2)}) collective-permute-start(f32[264,128]{1,0:T(8,128)S(1)} %get-tuple-element.26), channel_id=1, source_target_pairs={{0,1022},{1,1023},{14,12},{15,13},{16,14},{17,15},{30,28},{31,29},... | collective-permute-start | bytes 405512 | tf_op jit(solution)/shard_map/ppermute | solution.py:249
  28.6 0.0 collective-permute-done.1.up2_ref
  28.6 0.0 collective-permute-done.up1_ref
  28.6 0.0 copy-done.1
  28.6 8.5 %collective-permute-done.5.last2_ref = f32[264,128]{1,0:T(8,128)S(1)} collective-permute-done((f32[264,128]{1,0:T(8,128)S(1)}, f32[264,128]{1,0:T(8,128)S(1)}, u32[]{:S(2)}, u32[]{:S(2)}) %collective-permute-start.5) | collective-permute-done | bytes 135200 | tf_op jit(solution)/shard_map/ppermute | solution.py:249
  37.1 0.0 collective-permute-done.4.last1_ref
  37.1 5.5 %purify_last.1 = f32[2,8,128,128]{3,2,1,0:T(8,128)} custom-call(f32[2,8,128,128]{3,2,1,0:T(8,128)S(1)} %copy-done.1, s32[8,128]{1,0:T(8,128)S(1)} %get-tuple-element.16.missing_ref.refs_1_, f32[1160,128]{1,0:T(8,128)S(1)} %get-tuple-element.19.refs_2_.up1_ref, f32[264,128]{1,0:T(8,128)S(1)} %get-tuple-element.20.refs_3_.up2_ref, ...), custom_call_target="tpu_custom_call", output_to_operand_aliasing={{}: (8, {})} | custom-call | tf_op jit(solution)/shard_map/purify_last/pallas_call | solution.py:310
  (3 shorter events, 0.0 us)
Async XLA Ops:
  0.0 1.2 %copy-start = (f32[2,8,128,128]{3,2,1,0:T(8,128)S(1)}, f32[2,8,128,128]{3,2,1,0:T(8,128)}, u32[]{:S(2)}) copy-start(f32[2,8,128,128]{3,2,1,0:T(8,128)} %blocks_ref.3) | copy-start | bytes 3145732
  1.2 0.7 %copy-start.2 = (s32[2,8]{1,0:T(2,128)S(1)}, s32[2,8]{1,0:T(2,128)}, u32[]{:S(2)}) copy-start(s32[2,8]{1,0:T(2,128)} %refs_1_.1) | copy-start | bytes 196
  2.1 26.4 %collective-permute-start = (f32[1160,128]{1,0:T(8,128)S(1)}, f32[1160,128]{1,0:T(8,128)S(1)}, u32[]{:S(2)}, u32[]{:S(2)}) collective-permute-start(f32[1160,128]{1,0:T(8,128)S(1)} %get-tuple-element.17), channel_id=1, source_target_pairs={{0,1},{1,2},{2,3},{3,4},{4,5},{5,6},{6,7},{7,8},{8,9},{9,10},{10,1... | collective-permute-start | bytes 1781768 | tf_op jit(solution)/shard_map/ppermute | solution.py:242
  4.1 13.1 %collective-permute-start.2 = (f32[776,128]{1,0:T(8,128)S(1)}, f32[776,128]{1,0:T(8,128)S(1)}, u32[]{:S(2)}, u32[]{:S(2)}) collective-permute-start(f32[776,128]{1,0:T(8,128)S(1)} %get-tuple-element.21.refs_2_), channel_id=1, source_target_pairs={{1,0},{2,1},{3,2},{4,3},{5,4},{6,5},{7,6},{8,7},{9,8},{10,9},{11,1... | collective-permute-start | bytes 1191944 | tf_op jit(solution)/shard_map/ppermute | solution.py:249
  7.8 4.8 %collective-permute-start.3 = (f32[264,128]{1,0:T(8,128)S(1)}, f32[264,128]{1,0:T(8,128)S(1)}, u32[]{:S(2)}, u32[]{:S(2)}) collective-permute-start(f32[264,128]{1,0:T(8,128)S(1)} %get-tuple-element.22.refs_3_), channel_id=1, source_target_pairs={{2,0},{3,1},{4,2},{5,3},{6,4},{7,5},{8,6},{9,7},{10,8},{11,9},{12,... | collective-permute-start | bytes 405512 | tf_op jit(solution)/shard_map/ppermute | solution.py:249
  8.5 20.1 %collective-permute-start.1 = (f32[264,128]{1,0:T(8,128)S(1)}, f32[264,128]{1,0:T(8,128)S(1)}, u32[]{:S(2)}, u32[]{:S(2)}) collective-permute-start(f32[264,128]{1,0:T(8,128)S(1)} %get-tuple-element.18.tri_in_ref), channel_id=1, source_target_pairs={{0,2},{1,3},{2,4},{3,5},{4,6},{5,7},{6,8},{7,9},{8,10},{9,11},{10,... | collective-permute-start | bytes 405512 | tf_op jit(solution)/shard_map/ppermute | solution.py:242
  17.3 19.9 %collective-permute-start.4 = (f32[776,128]{1,0:T(8,128)S(1)}, f32[776,128]{1,0:T(8,128)S(1)}, u32[]{:S(2)}, u32[]{:S(2)}) collective-permute-start(f32[776,128]{1,0:T(8,128)S(1)} %get-tuple-element.25), channel_id=1, source_target_pairs={{0,1023},{16,15},{32,31},{48,47},{64,63},{80,79},{96,95},{112,111}... | collective-permute-start | bytes 1191944 | tf_op jit(solution)/shard_map/ppermute | solution.py:249
  17.9 10.6 %copy-start.1 = (f32[2,8,128,128]{3,2,1,0:T(8,128)S(1)}, f32[2,8,128,128]{3,2,1,0:T(8,128)}, u32[]{:S(2)}) copy-start(f32[2,8,128,128]{3,2,1,0:T(8,128)} %blocks_ref.3) | copy-start | bytes 3145732
  18.0 19.2 %collective-permute-start.5 = (f32[264,128]{1,0:T(8,128)S(1)}, f32[264,128]{1,0:T(8,128)S(1)}, u32[]{:S(2)}, u32[]{:S(2)}) collective-permute-start(f32[264,128]{1,0:T(8,128)S(1)} %get-tuple-element.26), channel_id=1, source_target_pairs={{0,1022},{1,1023},{14,12},{15,13},{16,14},{17,15},{30,28},{31,29},... | collective-permute-start | bytes 405512 | tf_op jit(solution)/shard_map/ppermute | solution.py:249

commit v4 on v3

--- a/solution.py
+++ b/solution.py
@@ -139,31 +139,6 @@
         put(k, j, value)
         put(j, k, value.T)
 
-    for i in range(ROWS):
-        for offset in range(2 * REACH + 1):
-            value = own_block(blocks_ref, missing, i, offset)
-            j = i + offset
-            if REACH <= j < REACH + ROWS:
-                put(REACH + i, j, value)
-            else:
-                put_both(REACH + i, j, value)
-    for ref, at in ((up2_ref, 0), (up1_ref, 2), (down1_ref, 6), (down2_ref, 8)):
-        first, between, second = read_triangle(ref)
-        put(at, at, first)
-        put_both(at, at + 1, between)
-        put(at + 1, at + 1, second)
-    for n, (k, j) in enumerate(((2, 0), (2, 1), (3, 0), (3, 1))):
-        put_both(k, j, up1_ref[PACKED + n * B : PACKED + (n + 1) * B])
-    for n, (k, j) in enumerate(((6, 8), (6, 9), (7, 8), (7, 9))):
-        put_both(k, j, down1_ref[PACKED + n * B : PACKED + (n + 1) * B])
-    for n, (k, j) in enumerate(((3, 6), (3, 7), (2, 6))):
-        put_both(k, j, up1_ref[DOWN + n * B : DOWN + (n + 1) * B])
-    nothing = jnp.zeros((B, B), BF)
-    for k, j in ((0, 5), (2, 7), (4, 9)):
-        for part in (high, low):
-            part[tile(k), tile(j)] = nothing
-            part[tile(j), tile(k)] = nothing
-
     def product(left_high, left_low, b):
         inner = slice(max(0, b - 2) * PAIR, min(SPAN // 2, b + 3) * PAIR)
         outer = slice(b * PAIR, (b + 1) * PAIR)
@@ -174,7 +149,7 @@
         return dot(left_high(inner), high) + dot(left_low(inner), high) + dot(left_high(inner), low)
 
     own = slice(REACH * B, (REACH + ROWS) * B)
-    for b in range(SPAN // 2):
+    def first_product(b):
         total = product(lambda at: high[own, at], lambda at: low[own, at], b)
         for i in range(ROWS):
             for j in (2 * b, 2 * b + 1):
@@ -188,6 +163,35 @@
                 top = value.astype(BF)
                 square_high[tile(i), tile(j)] = top
                 square_low[tile(i), tile(j)] = (value - top.astype(F32)).astype(BF)
+
+    nothing = jnp.zeros((B, B), BF)
+    for k, j in ((0, 5), (2, 7), (4, 9)):
+        for part in (high, low):
+            part[tile(k), tile(j)] = nothing
+            part[tile(j), tile(k)] = nothing
+
+    for i in range(ROWS):
+        for offset in range(2 * REACH + 1):
+            value = own_block(blocks_ref, missing, i, offset)
+            j = i + offset
+            if REACH <= j < REACH + ROWS:
+                put(REACH + i, j, value)
+            else:
+                put_both(REACH + i, j, value)
+    first_product(2)
+    for ref, at in ((up2_ref, 0), (up1_ref, 2), (down1_ref, 6), (down2_ref, 8)):
+        first, between, second = read_triangle(ref)
+        put(at, at, first)
+        put_both(at, at + 1, between)
+        put(at + 1, at + 1, second)
+    for n, (k, j) in enumerate(((2, 0), (2, 1), (3, 0), (3, 1))):
+        put_both(k, j, up1_ref[PACKED + n * B : PACKED + (n + 1) * B])
+    for n, (k, j) in enumerate(((6, 8), (6, 9), (7, 8), (7, 9))):
+        put_both(k, j, down1_ref[PACKED + n * B : PACKED + (n + 1) * B])
+    for n, (k, j) in enumerate(((3, 6), (3, 7), (2, 6))):
+        put_both(k, j, up1_ref[DOWN + n * B : DOWN + (n + 1) * B])
+    for b in (1, 3, 0, 4):
+        first_product(b)
     for b in range(SPAN // 2):
         total = product(lambda at: square_high[:, at], lambda at: square_low[:, at], b)
         outer = slice(b * PAIR, (b + 1) * PAIR)

time: 42.9 us -> 43 us (level)
  the two profiles are of different devices: /device:TPU:984 before, /device:TPU:986 now
where the time goes in v4:
time: 43 us; the launch traced here: 42.8 us
  starting transfers between devices  21.6 us (50%)
  waiting for transfers between devices  13.2 us (31%)
  Pallas kernels  5.93 us (14%)
  local copies, waits for them, and re-layouts  1.91 us (4%)
    ppermute x4, starting transfers between devices, shifted_down(): return lax.ppermute(value, AXES, pairs)  15.6 us
    ppermute x4, waiting for transfers between devices, shifted_down(): return lax.ppermute(value, AXES, pairs)  13.2 us
    ppermute x2, starting transfers between devices, shifted(): lax.ppermute(value, AXES, [(d, (d + by) % devices) for d in range(devices)])  6.02 us
    pallas_call x1, Pallas kernels, on_device(): pl.pallas_call(purify_last, out_shape=f32(ROWS, NNZ, B, B), in_specs=[VME...  5.62 us
    unnamed x6, local copies, waits for them, and re-layouts  1.91 us
  transfers between devices with their start and end apart: 6, of which 2 were waited for; matrix products, arithmetic and copies ran while one was open for 0% of the time, Pallas kernels for 0%

profile of v4, /device:TPU:986, one launch (start us, length us, event | category | flops | bytes accessed | tf_op | source)
XLA Modules:
  0.0 42.8 jit_solution(13293279840279541899)
XLA Ops:
  0.0 0.0 copy-start
  0.0 1.2 %copy-done = f32[2,8,128,128]{3,2,1,0:T(8,128)S(1)} copy-done((f32[2,8,128,128]{3,2,1,0:T(8,128)S(1)}, f32[2,8,128,128]{3,2,1,0:T(8,128)}, u32[]{:S(2)}) %copy-start) | copy-done | bytes 1048600
  1.2 0.0 copy-start.2
  1.2 0.7 %copy-done.2 = s32[2,8]{1,0:T(2,128)S(1)} copy-done((s32[2,8]{1,0:T(2,128)S(1)}, s32[2,8]{1,0:T(2,128)}, u32[]{:S(2)}) %copy-start.2) | copy-done | bytes 88
  1.9 0.2 pack_up.1
  2.1 1.9 %collective-permute-start = (f32[1160,128]{1,0:T(8,128)S(1)}, f32[1160,128]{1,0:T(8,128)S(1)}, u32[]{:S(2)}, u32[]{:S(2)}) collective-permute-start(f32[1160,128]{1,0:T(8,128)S(1)} %get-tuple-element.17), channel_id=1, source_target_pairs={{0,1},{1,2},{2,3},{3,4},{4,5},{5,6},{6,7},{7,8},{8,9},{9,10},{10,1... | collective-permute-start | bytes 1781768 | tf_op jit(solution)/shard_map/ppermute | solution.py:246
  4.0 0.1 pack_down.1
  4.1 3.6 %collective-permute-start.2 = (f32[776,128]{1,0:T(8,128)S(1)}, f32[776,128]{1,0:T(8,128)S(1)}, u32[]{:S(2)}, u32[]{:S(2)}) collective-permute-start(f32[776,128]{1,0:T(8,128)S(1)} %get-tuple-element.21.refs_2_), channel_id=1, source_target_pairs={{1,0},{2,1},{3,2},{4,3},{5,4},{6,5},{7,6},{8,7},{9,8},{10,9},{11,1... | collective-permute-start | bytes 1191944 | tf_op jit(solution)/shard_map/ppermute | solution.py:253
  7.8 0.7 %collective-permute-start.3 = (f32[264,128]{1,0:T(8,128)S(1)}, f32[264,128]{1,0:T(8,128)S(1)}, u32[]{:S(2)}, u32[]{:S(2)}) collective-permute-start(f32[264,128]{1,0:T(8,128)S(1)} %get-tuple-element.22.refs_3_), channel_id=1, source_target_pairs={{2,0},{3,1},{4,2},{5,3},{6,4},{7,5},{8,6},{9,7},{10,8},{11,9},{12,... | collective-permute-start | bytes 405512 | tf_op jit(solution)/shard_map/ppermute | solution.py:253
  8.5 4.1 %collective-permute-start.1 = (f32[264,128]{1,0:T(8,128)S(1)}, f32[264,128]{1,0:T(8,128)S(1)}, u32[]{:S(2)}, u32[]{:S(2)}) collective-permute-start(f32[264,128]{1,0:T(8,128)S(1)} %get-tuple-element.18.tri_in_ref), channel_id=1, source_target_pairs={{0,2},{1,3},{2,4},{3,5},{4,6},{5,7},{6,8},{7,9},{8,10},{9,11},{10,... | collective-permute-start | bytes 405512 | tf_op jit(solution)/shard_map/ppermute | solution.py:246
  12.6 0.0 collective-permute-done.3.refs_1_
  12.6 4.7 %collective-permute-done.2.refs_0_ = f32[776,128]{1,0:T(8,128)S(1)} collective-permute-done((f32[776,128]{1,0:T(8,128)S(1)}, f32[776,128]{1,0:T(8,128)S(1)}, u32[]{:S(2)}, u32[]{:S(2)}) %collective-permute-start.2) | collective-permute-done | bytes 397344 | tf_op jit(solution)/shard_map/ppermute | solution.py:253
  17.3 0.7 %collective-permute-start.4 = (f32[776,128]{1,0:T(8,128)S(1)}, f32[776,128]{1,0:T(8,128)S(1)}, u32[]{:S(2)}, u32[]{:S(2)}) collective-permute-start(f32[776,128]{1,0:T(8,128)S(1)} %get-tuple-element.25), channel_id=1, source_target_pairs={{0,1023},{16,15},{32,31},{48,47},{64,63},{80,79},{96,95},{112,111}... | collective-permute-start | bytes 1191944 | tf_op jit(solution)/shard_map/ppermute | solution.py:253
  17.9 0.0 copy-start.1
  18.0 10.6 %collective-permute-start.5 = (f32[264,128]{1,0:T(8,128)S(1)}, f32[264,128]{1,0:T(8,128)S(1)}, u32[]{:S(2)}, u32[]{:S(2)}) collective-permute-start(f32[264,128]{1,0:T(8,128)S(1)} %get-tuple-element.26), channel_id=1, source_target_pairs={{0,1022},{1,1023},{14,12},{15,13},{16,14},{17,15},{30,28},{31,29},... | collective-permute-start | bytes 405512 | tf_op jit(solution)/shard_map/ppermute | solution.py:253
  28.6 0.0 collective-permute-done.1.up2_ref
  28.6 0.0 collective-permute-done.up1_ref
  28.6 0.0 copy-done.1
  28.6 8.5 %collective-permute-done.5.last2_ref = f32[264,128]{1,0:T(8,128)S(1)} collective-permute-done((f32[264,128]{1,0:T(8,128)S(1)}, f32[264,128]{1,0:T(8,128)S(1)}, u32[]{:S(2)}, u32[]{:S(2)}) %collective-permute-start.5) | collective-permute-done | bytes 135200 | tf_op jit(solution)/shard_map/ppermute | solution.py:253
  37.1 0.0 collective-permute-done.4.last1_ref
  37.1 5.6 %purify_last.1 = f32[2,8,128,128]{3,2,1,0:T(8,128)} custom-call(f32[2,8,128,128]{3,2,1,0:T(8,128)S(1)} %copy-done.1, s32[8,128]{1,0:T(8,128)S(1)} %get-tuple-element.16.missing_ref.refs_1_, f32[1160,128]{1,0:T(8,128)S(1)} %get-tuple-element.19.refs_2_.up1_ref, f32[264,128]{1,0:T(8,128)S(1)} %get-tuple-element.20.refs_3_.up2_ref, ...), custom_call_target="tpu_custom_call", output_to_operand_aliasing={{}: (8, {})} | custom-call | tf_op jit(solution)/shard_map/purify_last/pallas_call | solution.py:314
  (3 shorter events, 0.0 us)
Async XLA Ops:
  0.0 1.2 %copy-start = (f32[2,8,128,128]{3,2,1,0:T(8,128)S(1)}, f32[2,8,128,128]{3,2,1,0:T(8,128)}, u32[]{:S(2)}) copy-start(f32[2,8,128,128]{3,2,1,0:T(8,128)} %blocks_ref.3) | copy-start | bytes 3145732
  1.2 0.7 %copy-start.2 = (s32[2,8]{1,0:T(2,128)S(1)}, s32[2,8]{1,0:T(2,128)}, u32[]{:S(2)}) copy-start(s32[2,8]{1,0:T(2,128)} %refs_1_.1) | copy-start | bytes 196
  2.1 26.4 %collective-permute-start = (f32[1160,128]{1,0:T(8,128)S(1)}, f32[1160,128]{1,0:T(8,128)S(1)}, u32[]{:S(2)}, u32[]{:S(2)}) collective-permute-start(f32[1160,128]{1,0:T(8,128)S(1)} %get-tuple-element.17), channel_id=1, source_target_pairs={{0,1},{1,2},{2,3},{3,4},{4,5},{5,6},{6,7},{7,8},{8,9},{9,10},{10,1... | collective-permute-start | bytes 1781768 | tf_op jit(solution)/shard_map/ppermute | solution.py:246
  4.1 13.1 %collective-permute-start.2 = (f32[776,128]{1,0:T(8,128)S(1)}, f32[776,128]{1,0:T(8,128)S(1)}, u32[]{:S(2)}, u32[]{:S(2)}) collective-permute-start(f32[776,128]{1,0:T(8,128)S(1)} %get-tuple-element.21.refs_2_), channel_id=1, source_target_pairs={{1,0},{2,1},{3,2},{4,3},{5,4},{6,5},{7,6},{8,7},{9,8},{10,9},{11,1... | collective-permute-start | bytes 1191944 | tf_op jit(solution)/shard_map/ppermute | solution.py:253
  7.8 4.8 %collective-permute-start.3 = (f32[264,128]{1,0:T(8,128)S(1)}, f32[264,128]{1,0:T(8,128)S(1)}, u32[]{:S(2)}, u32[]{:S(2)}) collective-permute-start(f32[264,128]{1,0:T(8,128)S(1)} %get-tuple-element.22.refs_3_), channel_id=1, source_target_pairs={{2,0},{3,1},{4,2},{5,3},{6,4},{7,5},{8,6},{9,7},{10,8},{11,9},{12,... | collective-permute-start | bytes 405512 | tf_op jit(solution)/shard_map/ppermute | solution.py:253
  8.5 20.1 %collective-permute-start.1 = (f32[264,128]{1,0:T(8,128)S(1)}, f32[264,128]{1,0:T(8,128)S(1)}, u32[]{:S(2)}, u32[]{:S(2)}) collective-permute-start(f32[264,128]{1,0:T(8,128)S(1)} %get-tuple-element.18.tri_in_ref), channel_id=1, source_target_pairs={{0,2},{1,3},{2,4},{3,5},{4,6},{5,7},{6,8},{7,9},{8,10},{9,11},{10,... | collective-permute-start | bytes 405512 | tf_op jit(solution)/shard_map/ppermute | solution.py:246
  17.3 19.9 %collective-permute-start.4 = (f32[776,128]{1,0:T(8,128)S(1)}, f32[776,128]{1,0:T(8,128)S(1)}, u32[]{:S(2)}, u32[]{:S(2)}) collective-permute-start(f32[776,128]{1,0:T(8,128)S(1)} %get-tuple-element.25), channel_id=1, source_target_pairs={{0,1023},{16,15},{32,31},{48,47},{64,63},{80,79},{96,95},{112,111}... | collective-permute-start | bytes 1191944 | tf_op jit(solution)/shard_map/ppermute | solution.py:253
  17.9 10.6 %copy-start.1 = (f32[2,8,128,128]{3,2,1,0:T(8,128)S(1)}, f32[2,8,128,128]{3,2,1,0:T(8,128)}, u32[]{:S(2)}) copy-start(f32[2,8,128,128]{3,2,1,0:T(8,128)} %blocks_ref.3) | copy-start | bytes 3145732
  18.0 19.2 %collective-permute-start.5 = (f32[264,128]{1,0:T(8,128)S(1)}, f32[264,128]{1,0:T(8,128)S(1)}, u32[]{:S(2)}, u32[]{:S(2)}) collective-permute-start(f32[264,128]{1,0:T(8,128)S(1)} %get-tuple-element.26), channel_id=1, source_target_pairs={{0,1022},{1,1023},{14,12},{15,13},{16,14},{17,15},{30,28},{31,29},... | collective-permute-start | bytes 405512 | tf_op jit(solution)/shard_map/ppermute | solution.py:253
